TPU v7x, 128 devices: a whole 4x4x4 slice. The times are simulated.
128 devices in a mesh: facet: 16 (over y_hi, x, core), dp: 8 (over z, y_lo).
Axes of the slice: x: 4, y: 4 (y_hi: 2, y_lo: 2; y = y_hi * 2 + y_lo), z: 4, core: 2. Of those that a mesh axis runs over, the one named last changes fastest.
Arguments:
- sky_image: float32 [128, 1024, 256], P('dp', 'facet'), as said below
- wave_dual: float32 [128, 1024, 256], P('dp', 'facet'), may hold values from -3 to 3
- rank_dual: float32 [128, 1024, 256], P('dp', 'facet'), may hold values from -3 to 3
- data_dual: float32 [16, 16, 1024, 256], P('facet', 'dp'), may hold values from -3 to 3
- observed: bfloat16 [16, 16, 1024, 256], P('facet', 'dp'), may hold values from -6 to 6
- radius: float32 [16, 16, 256], P('facet', 'dp'), may hold values from 20 to 400
- degrid: bfloat16 [16, 16, 24, 1024, 128], P('facet', 'dp'), may hold values from -0.15625 to 0.15625
- tile_list: int32 [16, 16, 24], P(None, 'dp'), may hold values from 0 to 127, as said below
- counts: int32 [16, 16], P(None, 'dp'), may hold values from 6 to 24
- keep_count: int32 [16], P('facet'), may hold values from 2 to 64
Outputs:
- sky_next: float32 [128, 1024, 256], P('dp', 'facet')
- wave_next: float32 [128, 1024, 256], P('dp', 'facet')
- rank_next: float32 [128, 1024, 256], P('dp', 'facet')
- data_next: float32 [16, 16, 1024, 256], P('facet', 'dp')
Inputs may be any that keep to these rules, and one draw needn't show every extreme that they name: `sky_image`: nonnegative. `tile_list`: A slot's value is f * 8 + t, tile t of source facet f in the block's band. Among the live slots of the 2 blocks of one device (facet g, band d) at most 3 name one source facet; in every band some source facet is named by exactly 3 live slots of every device of that band.
All inputs are finite; a program needn't handle non-finite values.
Results may differ from a plain program's by a relative error of at most 0.005.
Values may be sent and summed in bfloat16 or wider, within the bound.
A program may use at most 128 MiB of HBM per device.

v0:
```python
import jax
import jax.numpy as jnp
from jax import lax
from jax.experimental import pallas as pl
from jax.experimental.pallas import tpu as pltpu
from jax.sharding import PartitionSpec as P

MESH = pl.DeviceIdType.MESH
F32 = jnp.float32
BF16 = jnp.bfloat16
HIGH = lax.Precision.HIGHEST

TAPS = (-0.12940952255126037, -0.2241438680420134, 0.8365163037378079, -0.48296291314453416)
FACETS = 16
DP = 8
CAP = 3
SLOTS = 48
TILES = 8
PIX = 128
CH = 256
VIS = 1024
H = 16
W = 64
EDGE = 8


def newton_scales(kappa, steps):
    start = 2.0 / (1.0 + kappa)
    rho = (kappa - 1.0) / (kappa + 1.0)
    scales = []
    for _ in range(steps):
        scales.append(2.0 / (2.0 - rho * rho))
        rho = rho * rho / (2.0 - rho * rho)
    return start, scales


START, SCALES = newton_scales(65.0, 8)


def facet_at(i, me):
    y, x, c = me // 8, (me // 2) % 4, me % 2
    y = (y + 1 - i // 8) % 2
    x = (x + 1 + (i // 2) % 4) % 4
    c = (c + 1 - i % 2) % 2
    return (y * 4 + x) * 2 + c


def kernel(
    tab, keep, tvec, radius, sky_h, wave_h, rank_h, dual_h, obs_h, deg_h,
    sky_o, wave_o, rank_o, data_o,
    deg, dual, obs, sky, rank, wpad, epad, half, send1, recv1, send2, recv2, bar,
    acr, acr2, cols, synth, mixed, pick, gram, gpart, gsend, gfull, amat, inv, wnext, snext, rnext, misfit,
    lsem, osem, s1, r1, s2, r2, hs, hr, gs, gr, as_, ar,
):
    me = lax.axis_index("facet")
    dp = lax.axis_index("dp")

    def local(n, src, dst):
        copy = pltpu.make_async_copy(src, dst, lsem.at[n])
        copy.start()
        return copy

    get_wave = local(0, wave_h, wpad.at[pl.ds(2, H)])
    get_dual = local(1, dual_h, dual)
    get_deg = [
        local(2 + q, deg_h.at[pl.ds(q * 12, 12)], deg.at[pl.ds(q * 12, 12)]) for q in range(4)
    ]
    get_sky = local(6, sky_h, sky)
    get_rank = local(7, rank_h, rank)
    get_obs = local(8, obs_h, obs)

    barrier = pltpu.get_barrier_semaphore()

    def greet_facet(i, carry):
        pl.semaphore_signal(barrier, inc=1, device_id={"facet": facet_at(i, me)}, device_id_type=MESH)
        return carry

    def greet_dp(i, carry):
        pl.semaphore_signal(barrier, inc=1, device_id={"dp": (dp + 1 + i) % DP}, device_id_type=MESH)
        return carry

    lax.fori_loop(0, FACETS - 1, greet_facet, 0)
    lax.fori_loop(0, DP - 1, greet_dp, 0)

    row = lax.broadcasted_iota(jnp.int32, (TILES * 16, SLOTS * 16), 0)
    lane = lax.broadcasted_iota(jnp.int32, (TILES * 16, SLOTS * 16), 1)
    hit = (tvec[...] == row // 16) & (row % 16 == lane % 16)
    pick[...] = jnp.where(hit, 1.0, 0.0).astype(BF16)

    @pl.when(dp == 0)
    def _():
        wpad[0:2] = jnp.zeros((2, W, CH), F32)
        epad[0:1] = jnp.zeros((1, W, CH), F32)

    @pl.when(dp == DP - 1)
    def _():
        wpad[18:19] = jnp.zeros((1, W, CH), F32)
        epad[17:19] = jnp.zeros((2, W, CH), F32)

    @pl.when(me == 0)
    def _():
        cols[4:6] = jnp.zeros((2, H, CH), F32)
        cols[10:11] = jnp.zeros((1, H, CH), F32)

    @pl.when(me == FACETS - 1)
    def _():
        cols[6:7] = jnp.zeros((1, H, CH), F32)
        cols[12:14] = jnp.zeros((2, H, CH), F32)

    pl.semaphore_wait(barrier, FACETS - 1 + DP - 1)

    def hop(n, src, dst, axis, to):
        return pltpu.make_async_remote_copy(
            src_ref=src, dst_ref=dst, send_sem=hs.at[n], recv_sem=hr.at[n],
            device_id={axis: to}, device_id_type=MESH,
        )

    down, up = (dp + 1) % DP, (dp + DP - 1) % DP
    right, left = (me + 1) % FACETS, (me + FACETS - 1) % FACETS
    hops = (
        (hop(0, wpad.at[pl.ds(16, 2)], wpad.at[pl.ds(0, 2)], "dp", down), dp < DP - 1, dp > 0),
        (hop(1, wpad.at[pl.ds(2, 1)], wpad.at[pl.ds(18, 1)], "dp", up), dp > 0, dp < DP - 1),
        (hop(2, cols.at[pl.ds(0, 2)], cols.at[pl.ds(4, 2)], "facet", right), me < FACETS - 1, me > 0),
        (hop(3, cols.at[pl.ds(2, 1)], cols.at[pl.ds(6, 1)], "facet", left), me > 0, me < FACETS - 1),
        (hop(4, epad.at[pl.ds(16, 1)], epad.at[pl.ds(0, 1)], "dp", down), dp < DP - 1, dp > 0),
        (hop(5, epad.at[pl.ds(1, 2)], epad.at[pl.ds(17, 2)], "dp", up), dp > 0, dp < DP - 1),
        (hop(6, cols.at[pl.ds(7, 1)], cols.at[pl.ds(10, 1)], "facet", right), me < FACETS - 1, me > 0),
        (hop(7, cols.at[pl.ds(8, 2)], cols.at[pl.ds(12, 2)], "facet", left), me > 0, me < FACETS - 1),
    )

    def hop_start(n):
        copy, sends, _ = hops[n]

        @pl.when(sends)
        def _():
            copy.start()

    def hop_arrive(n):
        copy, _, receives = hops[n]

        @pl.when(receives)
        def _():
            copy.wait_recv()

    def hop_left(n):
        copy, sends, _ = hops[n]

        @pl.when(sends)
        def _():
            copy.wait_send()

    get_wave.wait()
    hop_start(0)
    hop_start(1)
    get_dual.wait()
    half[...] = dual[...].astype(BF16)
    for copy in get_deg:
        copy.wait()

    def out_1(to):
        return pltpu.make_async_remote_copy(
            src_ref=send1.at[pl.ds(to * CAP, CAP)], dst_ref=recv1.at[pl.ds(me * CAP, CAP)],
            send_sem=s1.at[to], recv_sem=r1.at[me], device_id={"facet": to}, device_id_type=MESH,
        )

    def in_1(source):
        return pltpu.make_async_remote_copy(
            src_ref=send1.at[pl.ds(source * CAP, CAP)], dst_ref=recv1.at[pl.ds(source * CAP, CAP)],
            send_sem=s1.at[source], recv_sem=r1.at[source], device_id={"facet": source},
            device_id_type=MESH,
        )

    def adjoint(i, carry):
        to = facet_at(i, me)
        for j in range(CAP):
            e = to * CAP + j
            weights = deg[tab[0, e]]
            rows = half[tab[6, e]]
            part = lax.dot_general(
                weights, rows, (((0,), (0,)), ((), ())), preferred_element_type=F32
            )
            send1[e] = (part * tab[1, e].astype(F32)).astype(BF16)

        @pl.when(i < FACETS - 1)
        def _():
            out_1(to).start()

        return carry

    lax.fori_loop(0, FACETS, adjoint, 0)
    recv1[pl.ds(me * CAP, CAP)] = send1[pl.ds(me * CAP, CAP)]

    hop_arrive(0)
    hop_arrive(1)

    def synth_rows(i, carry):
        total = TAPS[0] * wpad[i + 3]
        for a in range(1, 4):
            total = total + TAPS[a] * wpad[i + 3 - a]
        acr[i, EDGE : EDGE + W] = total
        return carry

    lax.fori_loop(0, H, synth_rows, 0)
    for q in range(2):
        cols[q] = acr[:, EDGE + W - 2 + q, :]
    cols[2] = acr[:, EDGE, :]
    hop_start(2)
    hop_start(3)
    get_sky.wait()
    get_rank.wait()
    hop_arrive(2)
    hop_arrive(3)
    for q in range(2):
        acr[:, EDGE - 2 + q, :] = cols[4 + q]
    acr[:, EDGE + W, :] = cols[6]

    def synth_cols(i, carry):
        total = TAPS[0] * acr[i, EDGE + 1 : EDGE + 1 + W]
        for a in range(1, 4):
            total = total + TAPS[a] * acr[i, EDGE + 1 - a : EDGE + 1 - a + W]
        synth[i] = total
        return carry

    lax.fori_loop(0, H, synth_cols, 0)

    def arrive_1(i, carry):
        in_1(facet_at(i, me)).wait_recv()
        return carry

    lax.fori_loop(0, FACETS - 1, arrive_1, 0)

    def update(i, carry):
        at = pl.multiple_of(i * 16, 16)
        tiles = recv1[:, pl.ds(at, 16), :].reshape(SLOTS * 16, CH)
        back = jnp.dot(pick[...], tiles, preferred_element_type=F32)
        for r in range(2):
            y = r * 8 + i
            held = sky[y]
            gradient = back[r * W : (r + 1) * W] + synth[y] + rank[y]
            after = jnp.maximum(held - 0.5 * gradient, 0.0)
            extrap = 2.0 * after - held
            snext[y] = after
            epad[y + 1] = extrap
            mixed[pl.ds(pl.multiple_of(y * W, W), W)] = rank[y] + 0.5 * extrap
            bar[r * 4 : r * 4 + 4, pl.ds(at, 16), :] = extrap.astype(BF16).reshape(4, 16, CH)
        return carry

    lax.fori_loop(0, 8, update, 0)
    put_sky = pltpu.make_async_copy(snext, sky_o, osem.at[0])
    put_sky.start()
    hop_start(4)
    hop_start(5)

    def out_2(to):
        return pltpu.make_async_remote_copy(
            src_ref=send2.at[pl.ds(to * CAP, CAP)], dst_ref=recv2.at[pl.ds(me * CAP, CAP)],
            send_sem=s2.at[to], recv_sem=r2.at[me], device_id={"facet": to}, device_id_type=MESH,
        )

    def in_2(source):
        return pltpu.make_async_remote_copy(
            src_ref=send2.at[pl.ds(source * CAP, CAP)], dst_ref=recv2.at[pl.ds(source * CAP, CAP)],
            send_sem=s2.at[source], recv_sem=r2.at[source], device_id={"facet": source},
            device_id_type=MESH,
        )

    def deal(i, carry):
        to = facet_at(i, me)
        for j in range(CAP):
            send2[to * CAP + j] = bar[tab[2, to * CAP + j]]

        @pl.when(i < FACETS - 1)
        def _():
            out_2(to).start()

        return carry

    lax.fori_loop(0, FACETS, deal, 0)
    recv2[pl.ds(me * CAP, CAP)] = send2[pl.ds(me * CAP, CAP)]

    rows_d = CH // DP
    gram[...] = lax.dot_general(
        mixed[...], mixed[...], (((0,), (0,)), ((), ())), precision=HIGH, preferred_element_type=F32
    ).reshape(DP, rows_d, CH)

    def gram_out(to):
        return pltpu.make_async_remote_copy(
            src_ref=gram.at[to], dst_ref=gpart.at[dp], send_sem=gs.at[to], recv_sem=gr.at[dp],
            device_id={"dp": to}, device_id_type=MESH,
        )

    def gram_in(source):
        return pltpu.make_async_remote_copy(
            src_ref=gram.at[source], dst_ref=gpart.at[source], send_sem=gs.at[source],
            recv_sem=gr.at[source], device_id={"dp": source}, device_id_type=MESH,
        )

    def all_out(to):
        return pltpu.make_async_remote_copy(
            src_ref=gsend, dst_ref=gfull.at[dp], send_sem=as_.at[to], recv_sem=ar.at[dp],
            device_id={"dp": to}, device_id_type=MESH,
        )

    def all_in(source):
        return pltpu.make_async_remote_copy(
            src_ref=gsend, dst_ref=gfull.at[source], send_sem=as_.at[source],
            recv_sem=ar.at[source], device_id={"dp": source}, device_id_type=MESH,
        )

    def others(fn):
        def step(i, carry):
            fn((dp + 1 + i) % DP)
            return carry

        lax.fori_loop(0, DP - 1, step, 0)

    others(lambda d: gram_out(d).start())
    gpart[dp] = gram[dp]

    hop_arrive(4)
    hop_arrive(5)

    def analysis_rows(i, carry):
        total = TAPS[0] * epad[i]
        for a in range(1, 4):
            total = total + TAPS[a] * epad[i + a]
        acr2[i, EDGE : EDGE + W] = total
        return carry

    lax.fori_loop(0, H, analysis_rows, 0)
    cols[7] = acr2[:, EDGE + W - 1, :]
    for q in range(2):
        cols[8 + q] = acr2[:, EDGE + q, :]
    hop_start(6)
    hop_start(7)

    others(lambda d: gram_in(d).wait_recv())
    total = gpart[0]
    for d in range(1, DP):
        total = total + gpart[d]
    gsend[...] = total
    others(lambda d: all_out(d).start())
    gfull[dp] = total

    hop_arrive(6)
    hop_arrive(7)
    acr2[:, EDGE - 1, :] = cols[10]
    for q in range(2):
        acr2[:, EDGE + W + q, :] = cols[12 + q]

    def analysis_cols(i, carry):
        total = TAPS[0] * acr2[i, EDGE - 1 : EDGE - 1 + W]
        for a in range(1, 4):
            total = total + TAPS[a] * acr2[i, EDGE - 1 + a : EDGE - 1 + a + W]
        wnext[i] = jnp.clip(wpad[i + 2] + 0.5 * total, -1.0, 1.0)
        return carry

    lax.fori_loop(0, H, analysis_cols, 0)
    put_wave = pltpu.make_async_copy(wnext, wave_o, osem.at[1])
    put_wave.start()

    others(lambda d: all_in(d).wait_recv())
    full = gfull[...].reshape(CH, CH)
    diag = lax.broadcasted_iota(jnp.int32, (CH, CH), 0) == lax.broadcasted_iota(jnp.int32, (CH, CH), 1)
    eye = jnp.where(diag, 1.0, 0.0)
    trace = jnp.sum(jnp.sum(full * eye, axis=1, keepdims=True), axis=0, keepdims=True)
    level = (trace + 1e-06) / keep[0].astype(F32)
    matrix = eye + full / level
    amat[...] = matrix
    inv[...] = (SCALES[0] * START) * (2.0 * eye - START * matrix)
    for scale in SCALES[1:]:
        x = inv[...]
        residual = 2.0 * eye - jnp.dot(amat[...], x, precision=HIGH, preferred_element_type=F32)
        inv[...] = scale * jnp.dot(x, residual, precision=HIGH, preferred_element_type=F32)

    def apply_rank(i, carry):
        at = pl.ds(pl.multiple_of(i * 256, 256), 256)
        out = jnp.dot(mixed[at], inv[...], precision=HIGH, preferred_element_type=F32)
        rnext[pl.ds(i * 4, 4)] = out.reshape(4, W, CH)
        return carry

    lax.fori_loop(0, 4, apply_rank, 0)
    put_rank = pltpu.make_async_copy(rnext, rank_o, osem.at[2])
    put_rank.start()

    def arrive_2(i, carry):
        in_2(facet_at(i, me)).wait_recv()
        return carry

    lax.fori_loop(0, FACETS - 1, arrive_2, 0)
    get_obs.wait()

    def gather(s, carry):
        send2[s] = (recv2[tab[4, s]].astype(F32) * tab[5, s].astype(F32)).astype(BF16)
        return carry

    def left_2(i, carry):
        out_2(facet_at(i, me)).wait_send()
        return carry

    lax.fori_loop(0, FACETS - 1, left_2, 0)
    lax.fori_loop(0, SLOTS, gather, 0)
    half_slots = SLOTS // 2
    puts = []
    for b in range(2):
        def forward(i, total, b=b):
            at = pl.ds(pl.multiple_of(i * 256, 256), 256)
            weights = jnp.concatenate(
                [deg[b * half_slots + s, at, :] for s in range(half_slots)], axis=1
            )
            tiles = send2[b * half_slots : (b + 1) * half_slots].reshape(half_slots * PIX, CH)
            model = jnp.dot(weights, tiles, preferred_element_type=F32)
            miss = dual[b, at, :] + model - obs[b, at, :].astype(F32)
            misfit[b, at, :] = miss
            return total + jnp.sum(miss * miss, axis=0, keepdims=True)

        total = lax.fori_loop(0, 4, forward, jnp.zeros((1, CH), F32))
        size = jnp.sqrt(total + 1e-06)
        shrink = jnp.maximum(0.0, 1.0 - radius[pl.ds(b, 1), :] / size)

        def scale_rows(i, carry, b=b, shrink=shrink):
            at = pl.ds(pl.multiple_of(i * 128, 128), 128)
            misfit[b, at, :] = misfit[b, at, :] * shrink
            return carry

        lax.fori_loop(0, 8, scale_rows, 0)
        put = pltpu.make_async_copy(misfit.at[b], data_o.at[b], osem.at[3 + b])
        put.start()
        puts.append(put)

    def left_1(i, carry):
        out_1(facet_at(i, me)).wait_send()
        return carry

    lax.fori_loop(0, FACETS - 1, left_1, 0)
    others(lambda d: gram_out(d).wait_send())
    others(lambda d: all_out(d).wait_send())
    for n in range(8):
        hop_left(n)
    put_sky.wait()
    put_wave.wait()
    put_rank.wait()
    for put in puts:
        put.wait()


def routing(tile_list, counts, me):
    flat = tile_list.reshape(FACETS, SLOTS)
    live = (jnp.arange(24)[None, None, :] < counts[:, :, None]).reshape(FACETS, SLOTS)
    source = jnp.where(live, flat // TILES, -1)
    mine = lax.dynamic_slice_in_dim(source, me, 1, 0)
    match = jnp.concatenate([mine == jnp.arange(FACETS)[:, None], source == me], axis=0)
    slot = jnp.arange(SLOTS)
    before = jnp.sum(
        jnp.where(match[:, None, :] & (slot[None, None, :] < slot[None, :, None]), 1, 0), axis=2
    )
    chosen = match[:, None, :] & (before[:, None, :] == jnp.arange(CAP)[None, :, None])
    value = jnp.concatenate([jnp.broadcast_to(slot[None], (FACETS, SLOTS)), flat % TILES], axis=0)
    picked = jnp.sum(jnp.where(chosen, value[:, None, :], 0), axis=2)
    there = jnp.sum(jnp.where(chosen, 1, 0), axis=2)
    entry = jnp.sum(
        jnp.where(match[:FACETS], jnp.arange(FACETS)[:, None] * CAP + before[:FACETS], 0), axis=0
    )
    mine_live = jnp.sum(jnp.where(match[:FACETS], 1, 0), axis=0)
    slots = picked[:FACETS].reshape(SLOTS)
    tiles = picked[FACETS:].reshape(SLOTS)
    tiles_live = there[FACETS:].reshape(SLOTS)
    table = jnp.stack(
        [
            slots, there[:FACETS].reshape(SLOTS), tiles, tiles_live, entry, mine_live, slots // 24,
            jnp.zeros_like(slots),
        ]
    ).astype(jnp.int32)
    spread = jnp.repeat(jnp.where(tiles_live > 0, tiles, -1), 16)[None].astype(jnp.int32)
    return table, spread


def per_device(
    sky_image, wave_dual, rank_dual, data_dual, observed, radius, degrid, tile_list, counts, keep_count
):
    me = lax.axis_index("facet")
    table, spread = routing(tile_list, counts, me)
    hbm = pl.BlockSpec(memory_space=pl.ANY)
    vmem = pl.BlockSpec(memory_space=pltpu.VMEM)
    smem = pl.BlockSpec(memory_space=pltpu.SMEM)
    dma = pltpu.SemaphoreType.DMA
    image = jax.ShapeDtypeStruct((H, W, CH), F32)
    outs = pl.pallas_call(
        kernel,
        out_shape=(image, image, image, jax.ShapeDtypeStruct((2, VIS, CH), F32)),
        in_specs=[smem, smem, vmem, vmem] + [hbm] * 6,
        out_specs=[hbm] * 4,
        scratch_shapes=[
            pltpu.VMEM((SLOTS, VIS, PIX), BF16),
            pltpu.VMEM((2, VIS, CH), F32),
            pltpu.VMEM((2, VIS, CH), BF16),
            pltpu.VMEM((H, W, CH), F32),
            pltpu.VMEM((H, W, CH), F32),
            pltpu.VMEM((H + 3, W, CH), F32),
            pltpu.VMEM((H + 3, W, CH), F32),
            pltpu.VMEM((2, VIS, CH), BF16),
            pltpu.VMEM((SLOTS, PIX, CH), BF16),
            pltpu.VMEM((SLOTS, PIX, CH), BF16),
            pltpu.VMEM((SLOTS, PIX, CH), BF16),
            pltpu.VMEM((SLOTS, PIX, CH), BF16),
            pltpu.VMEM((TILES, PIX, CH), BF16),
            pltpu.VMEM((H, W + 2 * EDGE, CH), F32),
            pltpu.VMEM((H, W + 2 * EDGE, CH), F32),
            pltpu.VMEM((14, H, CH), F32),
            pltpu.VMEM((H, W, CH), F32),
            pltpu.VMEM((H * W, CH), F32),
            pltpu.VMEM((TILES * 16, SLOTS * 16), BF16),
            pltpu.VMEM((DP, CH // DP, CH), F32),
            pltpu.VMEM((DP, CH // DP, CH), F32),
            pltpu.VMEM((CH // DP, CH), F32),
            pltpu.VMEM((DP, CH // DP, CH), F32),
            pltpu.VMEM((CH, CH), F32),
            pltpu.VMEM((CH, CH), F32),
            pltpu.VMEM((H, W, CH), F32),
            pltpu.VMEM((H, W, CH), F32),
            pltpu.VMEM((H, W, CH), F32),
            pltpu.VMEM((2, VIS, CH), F32),
            dma((9,)),
            dma((5,)),
            dma((FACETS,)),
            dma((FACETS,)),
            dma((FACETS,)),
            dma((FACETS,)),
            dma((8,)),
            dma((8,)),
            dma((DP,)),
            dma((DP,)),
            dma((DP,)),
            dma((DP,)),
        ],
        compiler_params=pltpu.CompilerParams(
            collective_id=0, has_side_effects=True, vmem_limit_bytes=60 * 1024 * 1024
        ),
    )(
        table, keep_count, spread, radius[0], sky_image, wave_dual, rank_dual, data_dual[0],
        observed[0], degrid.reshape(SLOTS, VIS, PIX),
    )
    return outs[0], outs[1], outs[2], outs[3][None]


def solution(mesh):
    return jax.shard_map(
        per_device,
        mesh=mesh,
        in_specs=(
            P("dp", "facet", None),
            P("dp", "facet", None),
            P("dp", "facet", None),
            P("facet", "dp", None, None),
            P("facet", "dp", None, None),
            P("facet", "dp", None),
            P("facet", "dp", None, None, None),
            P(None, "dp", None),
            P(None, "dp"),
            P("facet"),
        ),
        out_specs=(
            P("dp", "facet", None),
            P("dp", "facet", None),
            P("dp", "facet", None),
            P("facet", "dp", None, None),
        ),
        check_vma=False,
    )
```

profile of v0, /device:TPU:2, one launch (start us, length us, event | category | flops | bytes accessed | tf_op | source)
XLA Modules:
  0.0 139.3 jit_solution(3547240742588862160)
XLA Ops:
  1.3 0.1 lt.48
  1.4 0.8 reshape.91
  2.2 0.8 copy.16
  3.0 0.1 lt.51
  3.2 0.6 select_reduce_fusion
  3.8 0.2 select_reduce_fusion.1
  4.0 0.1 select_reduce_fusion.3
  4.2 0.1 copy.21
  4.3 0.1 select_n.68
  4.4 0.1 copy.19
  4.5 0.1 stack_reshape.14
  4.6 0.1 copy.17
  4.6 0.1 stack_reshape.12
  4.8 0.1 copy.20
  4.8 0.1 stack_reshape.15
  4.9 0.1 copy.18
  5.0 0.1 stack_reshape.13
  5.1 0.6 stack.12.tab
  5.8 0.7 broadcast_in_dim_reshape.3.tvec
  6.5 127.1 %shard_map.129 = (f32[16,64,256]{2,1,0:T(8,128)}, f32[16,64,256]{2,1,0:T(8,128)}, f32[16,64,256]{2,1,0:T(8,128)}, f32[2,1024,256]{2,1,0:T(8,128)}) custom-call(s32[8,48]{1,0:T(8,128)} %stack.12.tab, s32[1]{0:T(128)S(6)} %copy.26.keep, s32[1,768]{1,0:T(1,128)} %broadcast_in_dim_reshape.3.tvec, f32[2,256]{1,0:T(2,128)} %bitcast.15, f32[16,64,256]{2,1,0:T(8,128)} %sky_h.1, ...), custom_call_target="tpu_custom_call" | custom-call | tf_op jit(solution)/shard_map/pallas_call | solution.py:488
  133.5 2.4 %copy.27 = f32[16,64,256]{2,1,0:T(8,128)} copy(f32[16,64,256]{2,1,0:T(8,128)} %get-tuple-element.27) | data formatting | bytes 2097152
  136.0 1.0 copy.28
  137.0 1.0 copy.29
  138.0 1.3 copy.30
  (21 shorter events, 0.4 us)
Async XLA Ops:
  133.5 2.5 %copy-start.2 = (f32[16,64,256]{2,1,0:T(8,128)S(1)}, f32[16,64,256]{2,1,0:T(8,128)}, u32[]{:S(2)}) copy-start(f32[16,64,256]{2,1,0:T(8,128)} %get-tuple-element.28) | copy-start | bytes 3145732
  133.5 3.4 %copy-start.1 = (f32[16,64,256]{2,1,0:T(8,128)S(1)}, f32[16,64,256]{2,1,0:T(8,128)}, u32[]{:S(2)}) copy-start(f32[16,64,256]{2,1,0:T(8,128)} %get-tuple-element.29) | copy-start | bytes 3145732
  136.0 2.0 %copy-start = (f32[2,1024,256]{2,1,0:T(8,128)S(1)}, f32[2,1024,256]{2,1,0:T(8,128)}, u32[]{:S(2)}) copy-start(f32[2,1024,256]{2,1,0:T(8,128)} %get-tuple-element.11) | copy-start | bytes 6291460
where the time goes:
time: 140 us; the launch traced here: 139 us
  Pallas kernels  127 us (91%)
  local copies, waits for them, and re-layouts  9.82 us (7%)
  between operations  1.41 us (1%)
    pallas_call x1, Pallas kernels, per_device(): pl.pallas_call(kernel, out_shape=(image, image, image, jax.ShapeDtypeStru...  127 us
    unnamed x11, local copies, waits for them, and re-layouts  6.53 us

commit v1 on v0

v1 whole, which is shorter than its diff:
```python
import jax
import jax.numpy as jnp
from jax import lax
from jax.experimental import pallas as pl
from jax.experimental.pallas import tpu as pltpu
from jax.sharding import PartitionSpec as P

MESH = pl.DeviceIdType.MESH
F32 = jnp.float32
BF16 = jnp.bfloat16
HIGH = lax.Precision.HIGHEST

TAPS = (-0.12940952255126037, -0.2241438680420134, 0.8365163037378079, -0.48296291314453416)
FACETS = 16
DP = 8
CAP = 3
SLOTS = 48
TILES = 8
PIX = 128
CH = 256
VIS = 1024
H = 16
W = 64
HALF = 128
ROW = 8
EDGE = 8


def newton_scales(kappa, steps):
    start = 2.0 / (1.0 + kappa)
    rho = (kappa - 1.0) / (kappa + 1.0)
    scales = []
    for _ in range(steps):
        scales.append(2.0 / (2.0 - rho * rho))
        rho = rho * rho / (2.0 - rho * rho)
    return start, scales


START, SCALES = newton_scales(65.0, 8)


def column_at(i, me):
    x, c = (me // 2) % 4, me % 2
    return ((x + 1 + i // 2) % 4) * 2 + (c + 1 - i % 2) % 2


def match_table(source, value, target):
    lane = lax.broadcasted_iota(jnp.int32, (FACETS, SLOTS // 2), 1)
    seen = jnp.zeros((FACETS, 1), jnp.int32)
    values = [jnp.zeros((FACETS, 1), jnp.int32)] * CAP
    there = [jnp.zeros((FACETS, 1), jnp.int32)] * CAP
    for b in range(2):
        match = jnp.where(source[b] == target, 1, 0)
        before = jnp.broadcast_to(seen, match.shape)
        for s in range(SLOTS // 2 - 1):
            before = before + jnp.where(lane > s, match[:, s : s + 1], 0)
        seen = seen + jnp.sum(match, axis=1, keepdims=True)
        for j in range(CAP):
            chosen = jnp.where(before == j, match, 0)
            values[j] = values[j] + jnp.sum(chosen * value[b], axis=1, keepdims=True)
            there[j] = there[j] + jnp.sum(chosen, axis=1, keepdims=True)
    return values, there


def kernel(
    counts, keep, tiles_in, radius, sky_h, wave_h, rank_h, dual_h, obs_h, deg_h,
    sky_o, wave_o, rank_o, data_o,
    deg, dual, obs, sky, rank, wpad, epad, half, send1, recv1, ysend, yrecv, send2, recv2, bar, pbar_0, pbar_1,
    tcat, acc, acr, acr2, cols, synth, mixed, pick, tabv, tab, gram, gpart, gsend, gfull, amat, inv,
    lsem, s1, r1, s2, r2, ys, yr, hs, hr, gs, gr, as_, ar,
):
    me = lax.axis_index("facet")
    dp = lax.axis_index("dp")
    pbar = (pbar_0, pbar_1)
    mrow, mcol = me // ROW, me % ROW
    orow = 1 - mrow
    partner = orow * ROW + mcol

    def local(n, src, dst):
        copy = pltpu.make_async_copy(src, dst, lsem.at[n])
        copy.start()
        return copy

    get_wave = local(0, wave_h, wpad.at[pl.ds(2, H)])
    get_dual = local(1, dual_h, dual)
    get_deg = [
        local(2 + n, deg_h.at[pl.ds(n * 12, 12)], deg.at[pl.ds(n * 12, 12)]) for n in range(4)
    ]
    get_sky = local(6, sky_h, sky)
    get_rank = local(7, rank_h, rank)
    get_obs = local(8, obs_h, obs)

    barrier = pltpu.get_barrier_semaphore()

    def greet(axis, to):
        pl.semaphore_signal(barrier, inc=1, device_id={axis: to}, device_id_type=MESH)

    def greet_row(i, carry):
        greet("facet", mrow * ROW + column_at(i, me))
        return carry

    def greet_dp(i, carry):
        greet("dp", (dp + 1 + i) % DP)
        return carry

    down, up = (dp + 1) % DP, (dp + DP - 1) % DP
    right, left = (me + 1) % FACETS, (me + FACETS - 1) % FACETS
    lax.fori_loop(0, ROW - 1, greet_row, 0)
    lax.fori_loop(0, DP - 1, greet_dp, 0)
    greet("facet", partner)
    greet("facet", right)
    greet("facet", left)

    lane24 = lax.broadcasted_iota(jnp.int32, (1, SLOTS // 2), 1)
    rows16 = lax.broadcasted_iota(jnp.int32, (FACETS, 1), 0)
    mine, slot, workers, local_tile = [], [], [], []
    for b in range(2):
        line = tiles_in[pl.ds(me, 1), b, :]
        line = jnp.where(lane24 < counts[b, me], line // TILES, -1)
        mine.append(jnp.broadcast_to(line, (FACETS, SLOTS // 2)))
        slot.append(jnp.broadcast_to(lane24 + b * (SLOTS // 2), (FACETS, SLOTS // 2)))
        eight = tiles_in[pl.ds(pl.multiple_of(mrow * ROW, ROW), ROW), b, :]
        both = jnp.concatenate([eight, eight], axis=0)
        limit = jnp.zeros((FACETS, 1), jnp.int32)
        for n in range(ROW):
            limit = jnp.where(rows16 % ROW == n, counts[b, mrow * ROW + n], limit)
        workers.append(jnp.where(lane24 < limit, both // TILES, -1))
        local_tile.append(both % TILES)
    slots, slots_there = match_table(mine, slot, rows16)
    tiles, tiles_there = match_table(workers, local_tile, jnp.where(rows16 < ROW, partner, me))
    lanes = lax.broadcasted_iota(jnp.int32, (FACETS, 128), 1)
    table = jnp.zeros((FACETS, 128), jnp.int32)
    for n, column in enumerate(slots + slots_there + tiles + tiles_there):
        table = jnp.where(lanes == n, column, table)
    tabv[...] = table
    put_tab = pltpu.make_async_copy(tabv, tab, lsem.at[9])
    put_tab.start()

    wide = ROW * CAP * 16
    row = lax.broadcasted_iota(jnp.int32, (TILES * 16, wide), 0)
    lane = lax.broadcasted_iota(jnp.int32, (TILES * 16, wide), 1)
    lane8 = lax.broadcasted_iota(jnp.int32, (ROW, wide), 1)
    row8 = lax.broadcasted_iota(jnp.int32, (ROW, wide), 0)
    for kind in range(2):
        named = jnp.zeros((1, wide), jnp.int32)
        for j in range(CAP):
            code = jnp.where(tiles_there[j] > 0, tiles[j] + 1, 0)[kind * ROW : (kind + 1) * ROW]
            here = (lane8 // 48 == row8) & ((lane8 % 48) // 16 == j)
            named = named + jnp.sum(jnp.where(here, code, 0), axis=0, keepdims=True)
        hit = (named - 1 == row // 16) & (row % 16 == lane % 16)
        pick[kind] = jnp.where(hit, 1.0, 0.0).astype(BF16)

    @pl.when(dp == 0)
    def _():
        wpad[0:2] = jnp.zeros((2, W, CH), F32)
        epad[0:1] = jnp.zeros((1, W, CH), F32)

    @pl.when(dp == DP - 1)
    def _():
        wpad[18:19] = jnp.zeros((1, W, CH), F32)
        epad[17:19] = jnp.zeros((2, W, CH), F32)

    @pl.when(me == 0)
    def _():
        cols[4:6] = jnp.zeros((2, H, CH), F32)
        cols[10:11] = jnp.zeros((1, H, CH), F32)

    @pl.when(me == FACETS - 1)
    def _():
        cols[6:7] = jnp.zeros((1, H, CH), F32)
        cols[12:14] = jnp.zeros((2, H, CH), F32)

    pl.semaphore_wait(barrier, ROW - 1 + DP - 1 + 3)

    def hop(n, src, dst, axis, to):
        return pltpu.make_async_remote_copy(
            src_ref=src, dst_ref=dst, send_sem=hs.at[n], recv_sem=hr.at[n],
            device_id={axis: to}, device_id_type=MESH,
        )

    hops = (
        (hop(0, wpad.at[pl.ds(16, 2)], wpad.at[pl.ds(0, 2)], "dp", down), dp < DP - 1, dp > 0),
        (hop(1, wpad.at[pl.ds(2, 1)], wpad.at[pl.ds(18, 1)], "dp", up), dp > 0, dp < DP - 1),
        (hop(2, cols.at[pl.ds(0, 2)], cols.at[pl.ds(4, 2)], "facet", right), me < FACETS - 1, me > 0),
        (hop(3, cols.at[pl.ds(2, 1)], cols.at[pl.ds(6, 1)], "facet", left), me > 0, me < FACETS - 1),
        (hop(4, epad.at[pl.ds(16, 1)], epad.at[pl.ds(0, 1)], "dp", down), dp < DP - 1, dp > 0),
        (hop(5, epad.at[pl.ds(1, 2)], epad.at[pl.ds(17, 2)], "dp", up), dp > 0, dp < DP - 1),
        (hop(6, cols.at[pl.ds(7, 1)], cols.at[pl.ds(10, 1)], "facet", right), me < FACETS - 1, me > 0),
        (hop(7, cols.at[pl.ds(8, 2)], cols.at[pl.ds(12, 2)], "facet", left), me > 0, me < FACETS - 1),
    )

    def hop_start(n):
        copy, sends, _ = hops[n]

        @pl.when(sends)
        def _():
            copy.start()

    def hop_arrive(n):
        copy, _, receives = hops[n]

        @pl.when(receives)
        def _():
            copy.wait_recv()

    def hop_left(n):
        copy, sends, _ = hops[n]

        @pl.when(sends)
        def _():
            copy.wait_send()

    get_wave.wait()
    hop_start(0)
    hop_start(1)
    get_dual.wait()
    half[...] = dual[...].astype(BF16)
    put_tab.wait()
    for copy in get_deg:
        copy.wait()

    def row_copy(sends, src, dst, to, sent, came):
        return pltpu.make_async_remote_copy(
            src_ref=src, dst_ref=dst, send_sem=sends[0].at[sent], recv_sem=sends[1].at[came],
            device_id={"facet": mrow * ROW + to}, device_id_type=MESH,
        )

    def target_row(kind):
        return mrow if kind == 1 else orow

    def out_1(g, kind, to):
        return row_copy(
            (s1, r1), send1.at[g, pl.ds((target_row(kind) * ROW + to) * CAP, CAP)],
            recv1.at[g, pl.ds((kind * ROW + mcol) * CAP, CAP)], to,
            (g * 2 + kind) * ROW + to, (g * 2 + kind) * ROW + mcol,
        )

    def in_1(g, kind, source):
        region = recv1.at[g, pl.ds((kind * ROW + source) * CAP, CAP)]
        n = (g * 2 + kind) * ROW + source
        return row_copy((s1, r1), region, region, source, n, n)

    def out_2(g, kind, to):
        return row_copy(
            (s2, r2), send2.at[g, pl.ds((kind * ROW + to) * CAP, CAP)],
            recv2.at[g, pl.ds((target_row(kind) * ROW + mcol) * CAP, CAP)], to,
            (g * 2 + kind) * ROW + to, (g * 2 + kind) * ROW + mcol,
        )

    def in_2(g, kind, source):
        region = recv2.at[g, pl.ds((target_row(kind) * ROW + source) * CAP, CAP)]
        n = (g * 2 + kind) * ROW + source
        return row_copy((s2, r2), region, region, source, n, n)

    def across(g, n, src, dst):
        return pltpu.make_async_remote_copy(
            src_ref=src.at[g], dst_ref=dst, send_sem=ys.at[n * 2 + g], recv_sem=yr.at[n * 2 + g],
            device_id={"facet": partner}, device_id_type=MESH,
        )

    def each(fn):
        def step(i, carry):
            fn(column_at(i, me))
            return carry

        lax.fori_loop(0, ROW - 1, step, 0)

    for kind in range(2):
        def adjoint(i, carry, kind=kind):
            to = column_at(i, me)
            facet = target_row(kind) * ROW + to
            for j in range(CAP):
                at = tab[facet, j]
                part = lax.dot_general(
                    deg[at], half[jnp.where(at < SLOTS // 2, 0, 1)],
                    (((0,), (0,)), ((), ())), preferred_element_type=F32,
                )
                part = (part * tab[facet, CAP + j].astype(F32)).astype(BF16)
                send1[0, facet * CAP + j] = part[:, :HALF]
                send1[1, facet * CAP + j] = part[:, HALF:]

            @pl.when(i < ROW - 1)
            def _():
                out_1(0, kind, to).start()

            return carry

        lax.fori_loop(0, ROW, adjoint, 0)
    for kind in range(2):
        each(lambda to, kind=kind: out_1(1, kind, to).start())
    for g in range(2):
        for kind in range(2):
            recv1[g, pl.ds((kind * ROW + mcol) * CAP, CAP)] = send1[
                g, pl.ds((target_row(kind) * ROW + mcol) * CAP, CAP)
            ]

    hop_arrive(0)
    hop_arrive(1)

    def synth_rows(i, carry):
        total = TAPS[0] * wpad[i + 3]
        for a in range(1, 4):
            total = total + TAPS[a] * wpad[i + 3 - a]
        acr[i, EDGE : EDGE + W] = total
        return carry

    lax.fori_loop(0, H, synth_rows, 0)
    for q in range(2):
        cols[q] = acr[:, EDGE + W - 2 + q, :]
    cols[2] = acr[:, EDGE, :]
    hop_start(2)
    hop_start(3)
    get_sky.wait()
    get_rank.wait()
    hop_arrive(2)
    hop_arrive(3)
    for q in range(2):
        acr[:, EDGE - 2 + q, :] = cols[4 + q]
    acr[:, EDGE + W, :] = cols[6]

    def synth_cols(i, carry):
        total = TAPS[0] * acr[i, EDGE + 1 : EDGE + 1 + W]
        for a in range(1, 4):
            total = total + TAPS[a] * acr[i, EDGE + 1 - a : EDGE + 1 - a + W]
        synth[i] = total
        return carry

    lax.fori_loop(0, H, synth_cols, 0)

    entries = ROW * CAP

    def relay(g):
        each(lambda source: in_1(g, 0, source).wait_recv())

        def step(i, carry):
            at = pl.ds(pl.multiple_of(i * 16, 16), 16)
            part = recv1[g, 0:entries, at, :].reshape(entries * 16, HALF)
            total = jnp.dot(pick[0], part, preferred_element_type=F32)
            ysend[g, :, at, :] = total.astype(BF16).reshape(TILES, 16, HALF)
            return carry

        lax.fori_loop(0, 8, step, 0)
        across(g, 0, ysend, yrecv.at[g]).start()

    def update(g):
        each(lambda source: in_1(g, 1, source).wait_recv())
        across(g, 0, ysend, yrecv.at[g]).wait_recv()
        ch = slice(g * HALF, (g + 1) * HALF)

        def step(i, carry):
            at = pl.ds(pl.multiple_of(i * 16, 16), 16)
            part = recv1[g, entries : 2 * entries, at, :].reshape(entries * 16, HALF)
            back = jnp.dot(pick[1], part, preferred_element_type=F32)
            back = back + yrecv[g, :, at, :].reshape(TILES * 16, HALF).astype(F32)
            for r in range(2):
                y = r * 8 + i
                held = sky[y, :, ch]
                gradient = back[r * W : (r + 1) * W] + synth[y, :, ch] + rank[y, :, ch]
                after = jnp.maximum(held - 0.5 * gradient, 0.0)
                extrap = 2.0 * after - held
                sky_o[y, :, ch] = after
                epad[y + 1, :, ch] = extrap
                mixed[pl.ds(pl.multiple_of(y * W, W), W), ch] = rank[y, :, ch] + 0.5 * extrap
                bar[g, r * 4 : r * 4 + 4, at, :] = extrap.astype(BF16).reshape(4, 16, HALF)
            return carry

        lax.fori_loop(0, 8, step, 0)
        across(g, 1, bar, pbar[g]).start()

    def deal(g, kind):
        held = bar.at[g] if kind == 1 else pbar[g]
        if kind == 0:
            across(g, 1, bar, pbar[g]).wait_recv()

        def step(i, carry):
            to = column_at(i, me)
            for j in range(CAP):
                tile = held[tab[kind * ROW + to, 2 * CAP + j]]
                send2[g, (kind * ROW + to) * CAP + j] = tile

            @pl.when(i < ROW - 1)
            def _():
                out_2(g, kind, to).start()

            return carry

        lax.fori_loop(0, ROW, step, 0)
        recv2[g, pl.ds((target_row(kind) * ROW + mcol) * CAP, CAP)] = send2[
            g, pl.ds((kind * ROW + mcol) * CAP, CAP)
        ]

    relay(0)
    update(0)
    deal(0, 1)
    relay(1)
    deal(0, 0)
    update(1)
    deal(1, 1)
    hop_start(4)
    hop_start(5)

    rows_d = CH // DP
    gram[...] = lax.dot_general(
        mixed[...], mixed[...], (((0,), (0,)), ((), ())), precision=HIGH, preferred_element_type=F32
    ).reshape(DP, rows_d, CH)

    def gram_out(to):
        return pltpu.make_async_remote_copy(
            src_ref=gram.at[to], dst_ref=gpart.at[dp], send_sem=gs.at[to], recv_sem=gr.at[dp],
            device_id={"dp": to}, device_id_type=MESH,
        )

    def gram_in(source):
        return pltpu.make_async_remote_copy(
            src_ref=gram.at[source], dst_ref=gpart.at[source], send_sem=gs.at[source],
            recv_sem=gr.at[source], device_id={"dp": source}, device_id_type=MESH,
        )

    def all_out(to):
        return pltpu.make_async_remote_copy(
            src_ref=gsend, dst_ref=gfull.at[dp], send_sem=as_.at[to], recv_sem=ar.at[dp],
            device_id={"dp": to}, device_id_type=MESH,
        )

    def all_in(source):
        return pltpu.make_async_remote_copy(
            src_ref=gsend, dst_ref=gfull.at[source], send_sem=as_.at[source],
            recv_sem=ar.at[source], device_id={"dp": source}, device_id_type=MESH,
        )

    def others(fn):
        def step(i, carry):
            fn((dp + 1 + i) % DP)
            return carry

        lax.fori_loop(0, DP - 1, step, 0)

    others(lambda d: gram_out(d).start())
    gpart[dp] = gram[dp]

    deal(1, 0)

    hop_arrive(4)
    hop_arrive(5)

    def analysis_rows(i, carry):
        total = TAPS[0] * epad[i]
        for a in range(1, 4):
            total = total + TAPS[a] * epad[i + a]
        acr2[i, EDGE : EDGE + W] = total
        return carry

    lax.fori_loop(0, H, analysis_rows, 0)
    cols[7] = acr2[:, EDGE + W - 1, :]
    for q in range(2):
        cols[8 + q] = acr2[:, EDGE + q, :]
    hop_start(6)
    hop_start(7)

    others(lambda d: gram_in(d).wait_recv())
    total = gpart[0]
    for d in range(1, DP):
        total = total + gpart[d]
    gsend[...] = total
    others(lambda d: all_out(d).start())
    gfull[dp] = total

    hop_arrive(6)
    hop_arrive(7)
    acr2[:, EDGE - 1, :] = cols[10]
    for q in range(2):
        acr2[:, EDGE + W + q, :] = cols[12 + q]

    def analysis_cols(i, carry):
        total = TAPS[0] * acr2[i, EDGE - 1 : EDGE - 1 + W]
        for a in range(1, 4):
            total = total + TAPS[a] * acr2[i, EDGE - 1 + a : EDGE - 1 + a + W]
        wave_o[i] = jnp.clip(wpad[i + 2] + 0.5 * total, -1.0, 1.0)
        return carry

    lax.fori_loop(0, H, analysis_cols, 0)

    def forward(g, kind):
        each(lambda source: in_2(g, kind, source).wait_recv())
        first = target_row(kind) * ROW

        def spread(i, carry):
            for j in range(CAP):
                at = tab[first + i, j]
                live = tab[first + i, CAP + j]
                tile = recv2[g, (first + i) * CAP + j].astype(F32)
                for b in range(2):
                    mask = live * (jnp.where(at < SLOTS // 2, 1 - b, b))
                    tcat[i * CAP + j, :, b * HALF : (b + 1) * HALF] = (
                        tile * mask.astype(F32)
                    ).astype(BF16)
            return carry

        lax.fori_loop(0, ROW, spread, 0)

        def multiply(i, carry):
            at = pl.ds(pl.multiple_of(i * 256, 256), 256)
            weights = jnp.concatenate(
                [deg[tab[first + n // CAP, n % CAP], at, :] for n in range(entries)], axis=1
            )
            product = jnp.dot(
                weights, tcat[...].reshape(entries * PIX, CH), preferred_element_type=F32
            )
            if kind == 1:
                acc[g, at, :] = product
                return carry
            product = acc[g, at, :] + product
            ch = slice(g * HALF, (g + 1) * HALF)
            squares = []
            for b in range(2):
                miss = (
                    dual[b, at, ch]
                    + product[:, b * HALF : (b + 1) * HALF]
                    - obs[b, at, ch].astype(F32)
                )
                data_o[b, at, ch] = miss
                squares.append(carry[b] + jnp.sum(miss * miss, axis=0, keepdims=True))
            return tuple(squares)

        if kind == 1:
            lax.fori_loop(0, 4, multiply, 0)
            return
        zero = jnp.zeros((1, HALF), F32)
        totals = lax.fori_loop(0, 4, multiply, (zero, zero))
        ch = slice(g * HALF, (g + 1) * HALF)
        for b in range(2):
            size = jnp.sqrt(totals[b] + 1e-06)
            shrink = jnp.maximum(0.0, 1.0 - radius[pl.ds(b, 1), ch] / size)

            def scale_rows(i, carry, b=b, shrink=shrink):
                at = pl.ds(pl.multiple_of(i * 128, 128), 128)
                data_o[b, at, ch] = data_o[b, at, ch] * shrink
                return carry

            lax.fori_loop(0, 8, scale_rows, 0)

    get_obs.wait()
    forward(0, 1)
    forward(0, 0)

    others(lambda d: all_in(d).wait_recv())
    full = gfull[...].reshape(CH, CH)
    diag = lax.broadcasted_iota(jnp.int32, (CH, CH), 0) == lax.broadcasted_iota(jnp.int32, (CH, CH), 1)
    eye = jnp.where(diag, 1.0, 0.0)
    trace = jnp.sum(jnp.sum(full * eye, axis=1, keepdims=True), axis=0, keepdims=True)
    level = (trace + 1e-06) / keep[0].astype(F32)
    matrix = eye + full / level
    amat[...] = matrix
    inv[...] = (SCALES[0] * START) * (2.0 * eye - START * matrix)
    for scale in SCALES[1:]:
        x = inv[...]
        residual = 2.0 * eye - jnp.dot(amat[...], x, precision=HIGH, preferred_element_type=F32)
        inv[...] = scale * jnp.dot(x, residual, precision=HIGH, preferred_element_type=F32)

    def apply_rank(i, carry):
        at = pl.ds(pl.multiple_of(i * 256, 256), 256)
        out = jnp.dot(mixed[at], inv[...], precision=HIGH, preferred_element_type=F32)
        rank_o[pl.ds(i * 4, 4)] = out.reshape(4, W, CH)
        return carry

    lax.fori_loop(0, 4, apply_rank, 0)

    forward(1, 1)
    forward(1, 0)

    for g in range(2):
        for kind in range(2):
            each(lambda to, g=g, kind=kind: out_1(g, kind, to).wait_send())
            each(lambda to, g=g, kind=kind: out_2(g, kind, to).wait_send())
        across(g, 0, ysend, yrecv.at[g]).wait_send()
        across(g, 1, bar, pbar[g]).wait_send()
    others(lambda d: gram_out(d).wait_send())
    others(lambda d: all_out(d).wait_send())
    for n in range(8):
        hop_left(n)


def per_device(
    sky_image, wave_dual, rank_dual, data_dual, observed, radius, degrid, tile_list, counts, keep_count
):
    hbm = pl.BlockSpec(memory_space=pl.ANY)
    vmem = pl.BlockSpec(memory_space=pltpu.VMEM)
    smem = pl.BlockSpec(memory_space=pltpu.SMEM)
    dma = pltpu.SemaphoreType.DMA
    outs = pl.pallas_call(
        kernel,
        out_shape=(
            pltpu.VMEM((H, W, CH), F32), pltpu.VMEM((H, W, CH), F32), pltpu.VMEM((H, W, CH), F32),
            pltpu.VMEM((2, VIS, CH), F32),
        ),
        in_specs=[smem, smem, vmem, vmem] + [hbm] * 6,
        out_specs=[vmem] * 4,
        scratch_shapes=[
            pltpu.VMEM((SLOTS, VIS, PIX), BF16),
            pltpu.VMEM((2, VIS, CH), F32),
            pltpu.VMEM((2, VIS, CH), BF16),
            pltpu.VMEM((H, W, CH), F32),
            pltpu.VMEM((H, W, CH), F32),
            pltpu.VMEM((H + 3, W, CH), F32),
            pltpu.VMEM((H + 3, W, CH), F32),
            pltpu.VMEM((2, VIS, CH), BF16),
            pltpu.VMEM((2, SLOTS, PIX, HALF), BF16),
            pltpu.VMEM((2, SLOTS, PIX, HALF), BF16),
            pltpu.VMEM((2, TILES, PIX, HALF), BF16),
            pltpu.VMEM((2, TILES, PIX, HALF), BF16),
            pltpu.VMEM((2, SLOTS, PIX, HALF), BF16),
            pltpu.VMEM((2, SLOTS, PIX, HALF), BF16),
            pltpu.VMEM((2, TILES, PIX, HALF), BF16),
            pltpu.VMEM((TILES, PIX, HALF), BF16),
            pltpu.VMEM((TILES, PIX, HALF), BF16),
            pltpu.VMEM((ROW * CAP, PIX, CH), BF16),
            pltpu.VMEM((2, VIS, CH), F32),
            pltpu.VMEM((H, W + 2 * EDGE, CH), F32),
            pltpu.VMEM((H, W + 2 * EDGE, CH), F32),
            pltpu.VMEM((14, H, CH), F32),
            pltpu.VMEM((H, W, CH), F32),
            pltpu.VMEM((H * W, CH), F32),
            pltpu.VMEM((2, TILES * 16, ROW * CAP * 16), BF16),
            pltpu.VMEM((FACETS, 128), jnp.int32),
            pltpu.SMEM((FACETS, 128), jnp.int32),
            pltpu.VMEM((DP, CH // DP, CH), F32),
            pltpu.VMEM((DP, CH // DP, CH), F32),
            pltpu.VMEM((CH // DP, CH), F32),
            pltpu.VMEM((DP, CH // DP, CH), F32),
            pltpu.VMEM((CH, CH), F32),
            pltpu.VMEM((CH, CH), F32),
            dma((10,)),
            dma((4 * ROW,)),
            dma((4 * ROW,)),
            dma((4 * ROW,)),
            dma((4 * ROW,)),
            dma((4,)),
            dma((4,)),
            dma((8,)),
            dma((8,)),
            dma((DP,)),
            dma((DP,)),
            dma((DP,)),
            dma((DP,)),
        ],
        compiler_params=pltpu.CompilerParams(
            collective_id=0, has_side_effects=True, vmem_limit_bytes=52 * 1024 * 1024
        ),
    )(
        counts.T, keep_count, tile_list, radius[0], sky_image, wave_dual, rank_dual, data_dual[0],
        observed[0], degrid.reshape(SLOTS, VIS, PIX),
    )
    return outs[0], outs[1], outs[2], outs[3][None]


def solution(mesh):
    return jax.shard_map(
        per_device,
        mesh=mesh,
        in_specs=(
            P("dp", "facet", None),
            P("dp", "facet", None),
            P("dp", "facet", None),
            P("facet", "dp", None, None),
            P("facet", "dp", None, None),
            P("facet", "dp", None),
            P("facet", "dp", None, None, None),
            P(None, "dp", None),
            P(None, "dp"),
            P("facet"),
        ),
        out_specs=(
            P("dp", "facet", None),
            P("dp", "facet", None),
            P("dp", "facet", None),
            P("facet", "dp", None, None),
        ),
        check_vma=False,
    )
```

time: 140 us -> 122 us (0.87)
  the two profiles are of different devices: /device:TPU:2 before, /device:TPU:1 now
where the time goes in v1:
time: 122 us
  Pallas kernels  116 us (95%)
  local copies, waits for them, and re-layouts  4.23 us (3%)
  between operations  1.29 us (1%)
    pallas_call x1, Pallas kernels, per_device(): pl.pallas_call(kernel, out_shape=(pltpu.VMEM((H, W, CH), F32), pltpu.VMEM...  116 us
    unnamed x4, local copies, waits for them, and re-layouts  4.23 us

profile of v1, /device:TPU:1, one launch (start us, length us, event | category | flops | bytes accessed | tf_op | source)
XLA Modules:
  0.0 121.6 jit_solution(12333379203636317776)
XLA Ops:
  1.3 116.1 %shard_map.129 = (f32[16,64,256]{2,1,0:T(8,128)S(1)}, f32[16,64,256]{2,1,0:T(8,128)S(1)}, f32[16,64,256]{2,1,0:T(8,128)S(1)}, f32[2,1024,256]{2,1,0:T(8,128)S(1)}) custom-call(s32[2,16]{1,0:T(2,128)} %bitcast.11, s32[1]{0:T(128)S(6)} %copy.22.keep, s32[16,2,24]{2,1,0:T(2,128)} %tiles_in.1, f32[2,256]{1,0:T(2,128)} %bitcast.10, f32[16,64,256]{2,1,0:T(8,128)} %sky_h.1, ...), custom_call_target="tpu_custom_call" | custom-call | tf_op jit(solution)/shard_map/pallas_call | solution.py:590
  117.4 1.0 copy.18
  118.4 1.0 copy.19
  119.3 1.0 copy.20
  120.3 1.3 %copy.21 = f32[1,2,1024,256]{3,2,1,0:T(8,128)} copy(f32[1,2,1024,256]{3,2,1,0:T(8,128)S(1)} %bitcast.6) | data formatting | bytes 4194304

commit v2 on v1

--- a/solution.py
+++ b/solution.py
@@ -37,6 +37,20 @@
 
 
 START, SCALES = newton_scales(65.0, 8)
+
+
+def halves(x):
+    high = x.astype(BF16)
+    return high, (x - high.astype(F32)).astype(BF16)
+
+
+def dot3(a, b):
+    (ah, al), (bh, bl) = halves(a), halves(b)
+    return (
+        jnp.dot(ah, bl, preferred_element_type=F32)
+        + jnp.dot(al, bh, preferred_element_type=F32)
+        + jnp.dot(ah, bh, preferred_element_type=F32)
+    )
 
 
 def column_at(i, me):
@@ -286,8 +300,6 @@
             return carry
 
         lax.fori_loop(0, ROW, adjoint, 0)
-    for kind in range(2):
-        each(lambda to, kind=kind: out_1(1, kind, to).start())
     for g in range(2):
         for kind in range(2):
             recv1[g, pl.ds((kind * ROW + mcol) * CAP, CAP)] = send1[
@@ -326,6 +338,13 @@
         return carry
 
     lax.fori_loop(0, H, synth_cols, 0)
+
+    def follow(kind, to):
+        out_1(0, kind, to).wait_send()
+        out_1(1, kind, to).start()
+
+    for kind in range(2):
+        each(lambda to, kind=kind: follow(kind, to))
 
     entries = ROW * CAP
 
@@ -389,97 +408,6 @@
             g, pl.ds((kind * ROW + mcol) * CAP, CAP)
         ]
 
-    relay(0)
-    update(0)
-    deal(0, 1)
-    relay(1)
-    deal(0, 0)
-    update(1)
-    deal(1, 1)
-    hop_start(4)
-    hop_start(5)
-
-    rows_d = CH // DP
-    gram[...] = lax.dot_general(
-        mixed[...], mixed[...], (((0,), (0,)), ((), ())), precision=HIGH, preferred_element_type=F32
-    ).reshape(DP, rows_d, CH)
-
-    def gram_out(to):
-        return pltpu.make_async_remote_copy(
-            src_ref=gram.at[to], dst_ref=gpart.at[dp], send_sem=gs.at[to], recv_sem=gr.at[dp],
-            device_id={"dp": to}, device_id_type=MESH,
-        )
-
-    def gram_in(source):
-        return pltpu.make_async_remote_copy(
-            src_ref=gram.at[source], dst_ref=gpart.at[source], send_sem=gs.at[source],
-            recv_sem=gr.at[source], device_id={"dp": source}, device_id_type=MESH,
-        )
-
-    def all_out(to):
-        return pltpu.make_async_remote_copy(
-            src_ref=gsend, dst_ref=gfull.at[dp], send_sem=as_.at[to], recv_sem=ar.at[dp],
-            device_id={"dp": to}, device_id_type=MESH,
-        )
-
-    def all_in(source):
-        return pltpu.make_async_remote_copy(
-            src_ref=gsend, dst_ref=gfull.at[source], send_sem=as_.at[source],
-            recv_sem=ar.at[source], device_id={"dp": source}, device_id_type=MESH,
-        )
-
-    def others(fn):
-        def step(i, carry):
-            fn((dp + 1 + i) % DP)
-            return carry
-
-        lax.fori_loop(0, DP - 1, step, 0)
-
-    others(lambda d: gram_out(d).start())
-    gpart[dp] = gram[dp]
-
-    deal(1, 0)
-
-    hop_arrive(4)
-    hop_arrive(5)
-
-    def analysis_rows(i, carry):
-        total = TAPS[0] * epad[i]
-        for a in range(1, 4):
-            total = total + TAPS[a] * epad[i + a]
-        acr2[i, EDGE : EDGE + W] = total
-        return carry
-
-    lax.fori_loop(0, H, analysis_rows, 0)
-    cols[7] = acr2[:, EDGE + W - 1, :]
-    for q in range(2):
-        cols[8 + q] = acr2[:, EDGE + q, :]
-    hop_start(6)
-    hop_start(7)
-
-    others(lambda d: gram_in(d).wait_recv())
-    total = gpart[0]
-    for d in range(1, DP):
-        total = total + gpart[d]
-    gsend[...] = total
-    others(lambda d: all_out(d).start())
-    gfull[dp] = total
-
-    hop_arrive(6)
-    hop_arrive(7)
-    acr2[:, EDGE - 1, :] = cols[10]
-    for q in range(2):
-        acr2[:, EDGE + W + q, :] = cols[12 + q]
-
-    def analysis_cols(i, carry):
-        total = TAPS[0] * acr2[i, EDGE - 1 : EDGE - 1 + W]
-        for a in range(1, 4):
-            total = total + TAPS[a] * acr2[i, EDGE - 1 + a : EDGE - 1 + a + W]
-        wave_o[i] = jnp.clip(wpad[i + 2] + 0.5 * total, -1.0, 1.0)
-        return carry
-
-    lax.fori_loop(0, H, analysis_cols, 0)
-
     def forward(g, kind):
         each(lambda source: in_2(g, kind, source).wait_recv())
         first = target_row(kind) * ROW
@@ -499,7 +427,7 @@
         lax.fori_loop(0, ROW, spread, 0)
 
         def multiply(i, carry):
-            at = pl.ds(pl.multiple_of(i * 256, 256), 256)
+            at = pl.ds(pl.multiple_of(i * 512, 512), 512)
             weights = jnp.concatenate(
                 [deg[tab[first + n // CAP, n % CAP], at, :] for n in range(entries)], axis=1
             )
@@ -523,10 +451,10 @@
             return tuple(squares)
 
         if kind == 1:
-            lax.fori_loop(0, 4, multiply, 0)
+            lax.fori_loop(0, 2, multiply, 0)
             return
         zero = jnp.zeros((1, HALF), F32)
-        totals = lax.fori_loop(0, 4, multiply, (zero, zero))
+        totals = lax.fori_loop(0, 2, multiply, (zero, zero))
         ch = slice(g * HALF, (g + 1) * HALF)
         for b in range(2):
             size = jnp.sqrt(totals[b] + 1e-06)
@@ -540,8 +468,99 @@
             lax.fori_loop(0, 8, scale_rows, 0)
 
     get_obs.wait()
+    relay(0)
+    update(0)
+    deal(0, 1)
+    relay(1)
+    deal(0, 0)
+    update(1)
+    deal(1, 1)
+    hop_start(4)
+    hop_start(5)
+
+    rows_d = CH // DP
+    high, low = halves(mixed[...])
+    first = lax.dot_general(high, high, (((0,), (0,)), ((), ())), preferred_element_type=F32)
+    second = lax.dot_general(high, low, (((0,), (0,)), ((), ())), preferred_element_type=F32)
+    gram[...] = (first + (second + second.T)).reshape(DP, rows_d, CH)
+
+    def gram_out(to):
+        return pltpu.make_async_remote_copy(
+            src_ref=gram.at[to], dst_ref=gpart.at[dp], send_sem=gs.at[to], recv_sem=gr.at[dp],
+            device_id={"dp": to}, device_id_type=MESH,
+        )
+
+    def gram_in(source):
+        return pltpu.make_async_remote_copy(
+            src_ref=gram.at[source], dst_ref=gpart.at[source], send_sem=gs.at[source],
+            recv_sem=gr.at[source], device_id={"dp": source}, device_id_type=MESH,
+        )
+
+    def all_out(to):
+        return pltpu.make_async_remote_copy(
+            src_ref=gsend, dst_ref=gfull.at[dp], send_sem=as_.at[to], recv_sem=ar.at[dp],
+            device_id={"dp": to}, device_id_type=MESH,
+        )
+
+    def all_in(source):
+        return pltpu.make_async_remote_copy(
+            src_ref=gsend, dst_ref=gfull.at[source], send_sem=as_.at[source],
+            recv_sem=ar.at[source], device_id={"dp": source}, device_id_type=MESH,
+        )
+
+    def others(fn):
+        def step(i, carry):
+            fn((dp + 1 + i) % DP)
+            return carry
+
+        lax.fori_loop(0, DP - 1, step, 0)
+
+    others(lambda d: gram_out(d).start())
+    gpart[dp] = gram[dp]
+
     forward(0, 1)
+    deal(1, 0)
     forward(0, 0)
+
+    hop_arrive(4)
+    hop_arrive(5)
+
+    def analysis_rows(i, carry):
+        total = TAPS[0] * epad[i]
+        for a in range(1, 4):
+            total = total + TAPS[a] * epad[i + a]
+        acr2[i, EDGE : EDGE + W] = total
+        return carry
+
+    lax.fori_loop(0, H, analysis_rows, 0)
+    cols[7] = acr2[:, EDGE + W - 1, :]
+    for q in range(2):
+        cols[8 + q] = acr2[:, EDGE + q, :]
+    hop_start(6)
+    hop_start(7)
+
+    others(lambda d: gram_in(d).wait_recv())
+    total = gpart[0]
+    for d in range(1, DP):
+        total = total + gpart[d]
+    gsend[...] = total
+    others(lambda d: all_out(d).start())
+    gfull[dp] = total
+
+    hop_arrive(6)
+    hop_arrive(7)
+    acr2[:, EDGE - 1, :] = cols[10]
+    for q in range(2):
+        acr2[:, EDGE + W + q, :] = cols[12 + q]
+
+    def analysis_cols(i, carry):
+        total = TAPS[0] * acr2[i, EDGE - 1 : EDGE - 1 + W]
+        for a in range(1, 4):
+            total = total + TAPS[a] * acr2[i, EDGE - 1 + a : EDGE - 1 + a + W]
+        wave_o[i] = jnp.clip(wpad[i + 2] + 0.5 * total, -1.0, 1.0)
+        return carry
+
+    lax.fori_loop(0, H, analysis_cols, 0)
 
     others(lambda d: all_in(d).wait_recv())
     full = gfull[...].reshape(CH, CH)
@@ -552,14 +571,20 @@
     matrix = eye + full / level
     amat[...] = matrix
     inv[...] = (SCALES[0] * START) * (2.0 * eye - START * matrix)
-    for scale in SCALES[1:]:
+    coarse = matrix.astype(BF16)
+    x = inv[...]
+    for scale in SCALES[1:5]:
+        residual = 2.0 * eye - jnp.dot(coarse, x.astype(BF16), preferred_element_type=F32)
+        x = scale * jnp.dot(x.astype(BF16), residual.astype(BF16), preferred_element_type=F32)
+    inv[...] = x
+    for _ in range(3):
         x = inv[...]
-        residual = 2.0 * eye - jnp.dot(amat[...], x, precision=HIGH, preferred_element_type=F32)
-        inv[...] = scale * jnp.dot(x, residual, precision=HIGH, preferred_element_type=F32)
+        residual = eye - dot3(amat[...], x)
+        inv[...] = x + dot3(x, residual)
 
     def apply_rank(i, carry):
         at = pl.ds(pl.multiple_of(i * 256, 256), 256)
-        out = jnp.dot(mixed[at], inv[...], precision=HIGH, preferred_element_type=F32)
+        out = dot3(mixed[at], inv[...])
         rank_o[pl.ds(i * 4, 4)] = out.reshape(4, W, CH)
         return carry
 
@@ -570,7 +595,8 @@
 
     for g in range(2):
         for kind in range(2):
-            each(lambda to, g=g, kind=kind: out_1(g, kind, to).wait_send())
+            if g == 1:
+                each(lambda to, kind=kind: out_1(1, kind, to).wait_send())
             each(lambda to, g=g, kind=kind: out_2(g, kind, to).wait_send())
         across(g, 0, ysend, yrecv.at[g]).wait_send()
         across(g, 1, bar, pbar[g]).wait_send()

time: 122 us -> 100 us (0.82)
  the two profiles are of different devices: /device:TPU:1 before, /device:TPU:56 now
where the time goes in v2:
time: 100 us
  Pallas kernels  94.7 us (95%)
  local copies, waits for them, and re-layouts  4.23 us (4%)
  between operations  1.29 us (1%)
    pallas_call x1, Pallas kernels, per_device(): pl.pallas_call(kernel, out_shape=(pltpu.VMEM((H, W, CH), F32), pltpu.VMEM...  94.7 us
    unnamed x4, local copies, waits for them, and re-layouts  4.23 us

profile of v2, /device:TPU:56, one launch (start us, length us, event | category | flops | bytes accessed | tf_op | source)
XLA Modules:
  0.0 100.2 jit_solution(15127342154070411001)
XLA Ops:
  1.3 94.7 %shard_map.129 = (f32[16,64,256]{2,1,0:T(8,128)S(1)}, f32[16,64,256]{2,1,0:T(8,128)S(1)}, f32[16,64,256]{2,1,0:T(8,128)S(1)}, f32[2,1024,256]{2,1,0:T(8,128)S(1)}) custom-call(s32[2,16]{1,0:T(2,128)} %bitcast.11, s32[1]{0:T(128)S(6)} %copy.22.keep, s32[16,2,24]{2,1,0:T(2,128)} %tiles_in.1, f32[2,256]{1,0:T(2,128)} %bitcast.10, f32[16,64,256]{2,1,0:T(8,128)} %sky_h.1, ...), custom_call_target="tpu_custom_call" | custom-call | tf_op jit(solution)/shard_map/pallas_call | solution.py:616
  96.0 1.0 copy.18
  96.9 1.0 copy.19
  97.9 1.0 copy.20
  98.9 1.3 %copy.21 = f32[1,2,1024,256]{3,2,1,0:T(8,128)} copy(f32[1,2,1024,256]{3,2,1,0:T(8,128)S(1)} %bitcast.6) | data formatting | bytes 4194304

commit v3 on v2

--- a/solution.py
+++ b/solution.py
@@ -55,7 +55,9 @@
 
 def column_at(i, me):
     x, c = (me // 2) % 4, me % 2
-    return ((x + 1 + i // 2) % 4) * 2 + (c + 1 - i % 2) % 2
+    k = i // 2
+    hop = 1 + k + (k * (3 - k) // 2) * (3 - 2 * k)
+    return ((x + hop) % 4) * 2 + (c + 1 - i % 2) % 2
 
 
 def match_table(source, value, target):
@@ -95,15 +97,10 @@
         copy.start()
         return copy
 
-    get_wave = local(0, wave_h, wpad.at[pl.ds(2, H)])
     get_dual = local(1, dual_h, dual)
     get_deg = [
         local(2 + n, deg_h.at[pl.ds(n * 12, 12)], deg.at[pl.ds(n * 12, 12)]) for n in range(4)
     ]
-    get_sky = local(6, sky_h, sky)
-    get_rank = local(7, rank_h, rank)
-    get_obs = local(8, obs_h, obs)
-
     barrier = pltpu.get_barrier_semaphore()
 
     def greet(axis, to):
@@ -224,14 +221,15 @@
         def _():
             copy.wait_send()
 
-    get_wave.wait()
-    hop_start(0)
-    hop_start(1)
     get_dual.wait()
     half[...] = dual[...].astype(BF16)
     put_tab.wait()
     for copy in get_deg:
         copy.wait()
+    get_wave = local(0, wave_h, wpad.at[pl.ds(2, H)])
+    get_sky = local(6, sky_h, sky)
+    get_rank = local(7, rank_h, rank)
+    get_obs = local(8, obs_h, obs)
 
     def row_copy(sends, src, dst, to, sent, came):
         return pltpu.make_async_remote_copy(
@@ -305,6 +303,10 @@
             recv1[g, pl.ds((kind * ROW + mcol) * CAP, CAP)] = send1[
                 g, pl.ds((target_row(kind) * ROW + mcol) * CAP, CAP)
             ]
+
+    get_wave.wait()
+    hop_start(0)
+    hop_start(1)
 
     hop_arrive(0)
     hop_arrive(1)
@@ -520,7 +522,6 @@
 
     forward(0, 1)
     deal(1, 0)
-    forward(0, 0)
 
     hop_arrive(4)
     hop_arrive(5)
@@ -547,6 +548,7 @@
     others(lambda d: all_out(d).start())
     gfull[dp] = total
 
+    forward(0, 0)
     hop_arrive(6)
     hop_arrive(7)
     acr2[:, EDGE - 1, :] = cols[10]
@@ -562,6 +564,7 @@
 
     lax.fori_loop(0, H, analysis_cols, 0)
 
+    forward(1, 1)
     others(lambda d: all_in(d).wait_recv())
     full = gfull[...].reshape(CH, CH)
     diag = lax.broadcasted_iota(jnp.int32, (CH, CH), 0) == lax.broadcasted_iota(jnp.int32, (CH, CH), 1)
@@ -573,14 +576,20 @@
     inv[...] = (SCALES[0] * START) * (2.0 * eye - START * matrix)
     coarse = matrix.astype(BF16)
     x = inv[...]
-    for scale in SCALES[1:5]:
+    for scale in SCALES[1:4]:
         residual = 2.0 * eye - jnp.dot(coarse, x.astype(BF16), preferred_element_type=F32)
         x = scale * jnp.dot(x.astype(BF16), residual.astype(BF16), preferred_element_type=F32)
-    inv[...] = x
-    for _ in range(3):
-        x = inv[...]
-        residual = eye - dot3(amat[...], x)
-        inv[...] = x + dot3(x, residual)
+    fine = (matrix - coarse.astype(F32)).astype(BF16)
+    x = x.astype(BF16)
+    residual = eye - (
+        jnp.dot(coarse, x, preferred_element_type=F32) + jnp.dot(fine, x, preferred_element_type=F32)
+    )
+    inv[...] = x.astype(F32) + jnp.dot(x, residual.astype(BF16), preferred_element_type=F32)
+    x = inv[...]
+    inv[...] = x + dot3(x, eye - dot3(amat[...], x))
+    x = inv[...]
+    residual = eye - dot3(amat[...], x)
+    inv[...] = x + jnp.dot(x.astype(BF16), residual.astype(BF16), preferred_element_type=F32)
 
     def apply_rank(i, carry):
         at = pl.ds(pl.multiple_of(i * 256, 256), 256)
@@ -590,7 +599,6 @@
 
     lax.fori_loop(0, 4, apply_rank, 0)
 
-    forward(1, 1)
     forward(1, 0)
 
     for g in range(2):

time: 100 us -> 97.8 us (0.978)
  the two profiles are of different devices: /device:TPU:56 before, /device:TPU:1 now
where the time goes in v3:
time: 97.8 us; the launch traced here: 97.7 us
  Pallas kernels  92.2 us (94%)
  local copies, waits for them, and re-layouts  4.23 us (4%)
  between operations  1.29 us (1%)
    pallas_call x1, Pallas kernels, per_device(): pl.pallas_call(kernel, out_shape=(pltpu.VMEM((H, W, CH), F32), pltpu.VMEM...  92.2 us
    unnamed x4, local copies, waits for them, and re-layouts  4.23 us

profile of v3, /device:TPU:1, one launch (start us, length us, event | category | flops | bytes accessed | tf_op | source)
XLA Modules:
  0.0 97.7 jit_solution(10419199242578692102)
XLA Ops:
  1.3 92.2 %shard_map.129 = (f32[16,64,256]{2,1,0:T(8,128)S(1)}, f32[16,64,256]{2,1,0:T(8,128)S(1)}, f32[16,64,256]{2,1,0:T(8,128)S(1)}, f32[2,1024,256]{2,1,0:T(8,128)S(1)}) custom-call(s32[2,16]{1,0:T(2,128)} %bitcast.11, s32[1]{0:T(128)S(6)} %copy.22.keep, s32[16,2,24]{2,1,0:T(2,128)} %tiles_in.1, f32[2,256]{1,0:T(2,128)} %bitcast.10, f32[16,64,256]{2,1,0:T(8,128)} %sky_h.1, ...), custom_call_target="tpu_custom_call" | custom-call | tf_op jit(solution)/shard_map/pallas_call | solution.py:624
  93.4 1.0 copy.18
  94.4 1.0 copy.19
  95.4 1.0 copy.20
  96.4 1.3 %copy.21 = f32[1,2,1024,256]{3,2,1,0:T(8,128)} copy(f32[1,2,1024,256]{3,2,1,0:T(8,128)S(1)} %bitcast.6) | data formatting | bytes 4194304
